TPU v7x, 32 devices: a whole 2x2x4 slice. The times are simulated.
32 devices in a mesh: dp: 4 (over y, x), feat: 8 (over z, core).
Axes of the slice: x: 2, y: 2, z: 4, core: 2. Of those that a mesh axis runs over, the one named last changes fastest.
Arguments:
- tokens: bfloat16 [512, 16384], P('dp', 'feat'), may hold values from -6 to 6
- columns: int32 [256, 16], P('feat'), may hold values from 0 to 127, all different within a row
- weight: bfloat16 [256, 16, 128, 128], P('feat', None, 'dp'), may hold values from -0.125 to 0.125
- cotangent: bfloat16 [512, 32768], P('dp', 'feat'), may hold values from -6 to 6
Outputs:
- hidden: bfloat16 [512, 32768], P('dp', 'feat')
- input_grad: bfloat16 [512, 16384], P('dp', 'feat')
- weight_grad: bfloat16 [256, 16, 128, 128], P('feat', None, 'dp')
Inputs may be any that keep to these rules, and one draw needn't show every extreme that they name: `columns`: the 16 entries of a row are distinct input blocks; every input block is named by some row.
All inputs are finite; a program needn't handle non-finite values.
Results may differ from a plain program's by a relative error of at most 0.019.
Values may be sent and summed in bfloat16 or wider, within the bound.
A program may use at most 128 MiB of HBM per device.

v0:
```python
import jax
import jax.numpy as jnp
from jax import lax
from jax.sharding import PartitionSpec as P


def gelu_tanh(value):
    return jax.nn.gelu(value, approximate=True)


def on_device(tokens, columns, weight, cotangent):
    tok_rows = tokens.shape[0]
    local_rows = weight.shape[0]
    slots = weight.shape[1]
    side = weight.shape[3]
    feat_count = lax.axis_size("feat")
    gathered = lax.all_gather(tokens, "feat", axis=1, tiled=True)
    block_count = gathered.shape[1] // side
    flat_cols = columns.reshape(-1)
    picked = gathered.reshape(tok_rows, block_count, side)[:, flat_cols, :].reshape(
        tok_rows, local_rows, slots, side
    )
    full_weight = lax.all_gather(weight, "dp", axis=2, tiled=True)
    pre = jnp.einsum("trsk,rsuk->tru", picked, full_weight, preferred_element_type=jnp.float32)
    act, pull = jax.vjp(gelu_tanh, pre)
    hidden = act.astype(jnp.bfloat16).reshape(tok_rows, local_rows * side)
    grad_pre = pull(cotangent.reshape(tok_rows, local_rows, side).astype(jnp.float32))[0].astype(
        jnp.bfloat16
    )
    weight_terms = jnp.einsum(
        "tru,trsk->rsuk", grad_pre, picked, preferred_element_type=jnp.float32
    )
    weight_grad = lax.psum_scatter(
        weight_terms.astype(jnp.bfloat16), "dp", scatter_dimension=2, tiled=True
    )
    partial_grad = jnp.einsum(
        "tru,rsuk->trsk", grad_pre, full_weight, preferred_element_type=jnp.float32
    )
    onehot = (flat_cols[:, None] == jnp.arange(block_count, dtype=jnp.int32)[None, :]).astype(
        jnp.float32
    )
    spread = jnp.einsum(
        "tqk,qb->tbk",
        partial_grad.reshape(tok_rows, local_rows * slots, side),
        onehot,
        precision=lax.Precision.HIGHEST,
    )
    outgoing = spread.reshape(tok_rows, block_count * side).astype(jnp.bfloat16)
    returned = lax.all_to_all(outgoing, "feat", split_axis=1, concat_axis=0, tiled=True)
    input_grad = jnp.sum(
        returned.reshape(feat_count, tok_rows, -1).astype(jnp.float32), axis=0
    ).astype(jnp.bfloat16)
    return (hidden, input_grad, weight_grad)


def solution(mesh):
    in_specs = (P("dp", "feat"), P("feat", None), P("feat", None, "dp", None), P("dp", "feat"))
    out_specs = (P("dp", "feat"), P("dp", "feat"), P("feat", None, "dp", None))
    return jax.shard_map(
        on_device, mesh=mesh, in_specs=in_specs, out_specs=out_specs, check_vma=False
    )
```

profile of v0, /device:TPU:18, one launch (start us, length us, event | category | flops | bytes accessed | tf_op | source)
XLA Modules:
  0.0 461.6 jit_solution(6730337653898310709)
XLA Ops:
  7.2 0.0 copy-start.2
  7.2 0.0 copy-start
  7.2 0.0 all-gather.3.cloned.1.call-start
  7.2 2.1 copy.35
  9.4 0.0 all-gather.3.cloned.1.call-update
  9.4 0.0 all-gather.5.cloned.1.call-start
  9.4 0.7 all-gather.5.cloned.1.call-update
  10.1 0.0 reduce-scatter.2.cloned.1.call-start
  10.2 0.0 copy-done.2
  10.2 0.1 copy.36
  10.3 0.1 reshape.62
  10.3 0.0 copy-done
  10.3 0.5 copy.39
  10.9 46.2 %all-gather.3.cloned.1.call-done = bf16[128,16384]{0,1:T(8,128)(2,1)} async-done(((bf16[128,2048]{0,1:T(8,128)(2,1)}), bf16[128,16384]{0,1:T(8,128)(2,1)}) %all-gather.3.cloned.1.call-update) | async-done | bytes 4194320 | tf_op jit(solution)/shard_map/all_gather | solution.py:17
  57.1 6.4 %copy.37 = bf16[128,128,128]{2,0,1:T(8,128)(2,1)} copy(bf16[128,128,128]{0,2,1:T(8,128)(2,1)} %bitcast.52) | data formatting | bytes 8388608 | tf_op jit(solution)/shard_map/reshape | solution.py:20
  63.4 16.2 %gather_fusion = bf16[512,128,128]{2,1,0:T(8,128)(2,1)} fusion(bf16[128,128,128]{2,0,1:T(8,128)(2,1)} %copy.37, s32[1024]{0:T(1024)S(1)} %pad_clamp_fusion), kind=kCustom, calls=%fused_computation | custom fusion | bytes 33556480 | tf_op jit(solution)/shard_map/gather | solution.py:20
  79.6 136.7 %all-gather.5.cloned.1.call-done = bf16[32,16,128,128]{3,2,1,0:T(8,128)(2,1)} async-done(((bf16[32,16,32,128]{3,2,1,0:T(8,128)(2,1)}), bf16[32,16,128,128]{3,2,1,0:T(8,128)(2,1)}) %all-gather.5.cloned.1.call-update) | async-done | bytes 16777232 | tf_op jit(solution)/shard_map/all_gather | solution.py:23
  216.2 14.2 %fusion.10 = (bf16[128,32,128]{0,2,1:T(8,128)(2,1)S(1)}, bf16[128,32,128]{0,2,1:T(8,128)(2,1)}) fusion(f32[128,32,128]{0,2,1:T(8,128)S(1)} %bitcast.53, bf16[128,32,16,128]{3,0,2,1:T(8,128)(2,1)} %bitcast.50, bf16[32,16,128,128]{3,2,1,0:T(8,128)(2,1)} %all-gather.5.cloned.1.call-done), kind=kOutput, calls=%fused_computation.13 | convolution fusion | flops 2159017984 | bytes 37748736 | tf_op jit(solution)/shard_map/trsk,rsuk->tru/dot_general | solution.py:24
  230.4 14.9 %convert_bitcast_fusion = bf16[32,16,128,128]{2,3,1,0:T(8,128)(2,1)} fusion(bf16[128,32,16,128]{3,0,2,1:T(8,128)(2,1)} %bitcast.51, bf16[128,32,128]{0,2,1:T(8,128)(2,1)S(1)} %get-tuple-element.15), kind=kOutput, calls=%fused_computation.3 | convolution fusion | flops 2155872256 | bytes 34603008 | tf_op jit(solution)/shard_map/tru,trsk->rsuk/dot_general | solution.py:30
  245.2 22.5 %copy.45 = bf16[32,16,128,128]{3,1,0,2:T(8,128)(2,1)} copy(bf16[32,16,128,128]{2,3,1,0:T(8,128)(2,1)} %convert_bitcast_fusion) | data formatting | bytes 33554432 | tf_op jit(solution)/shard_map/convert_element_type | solution.py:34
  267.7 0.0 reduce-scatter.2.cloned.1.call-update
  267.7 0.1 eq.15
  267.8 22.5 %fusion.15 = f32[32,128,16,128]{3,1,2,0:T(8,128)} fusion(bf16[32,16,128,128]{3,2,1,0:T(8,128)(2,1)} %all-gather.5.cloned.1.call-done, bf16[128,32,128]{0,2,1:T(8,128)(2,1)S(1)} %get-tuple-element.15), kind=kOutput, calls=%fused_computation.20 | convolution fusion | flops 2147483648 | bytes 51380224 | tf_op jit(solution)/shard_map/tru,rsuk->trsk/dot_general | solution.py:36
  290.3 41.9 %convert_bitcast_fusion.1 = bf16[128,128,128]{2,1,0:T(8,128)(2,1)} fusion(f32[128,512,128]{2,0,1:T(8,128)} %bitcast.49, s32[512]{0:T(512)S(1)} %eq.15), kind=kOutput, calls=%fused_computation.4 | convolution fusion | flops 12887064576 | bytes 37750784 | tf_op jit(solution)/shard_map/tqk,qb->tbk/dot_general | solution.py:42
  332.1 7.4 %convert_element_type.37 = bf16[128,8,2048]{2,1,0:T(8,128)(2,1)} reshape(bf16[128,128,128]{2,1,0:T(8,128)(2,1)} %convert_bitcast_fusion.1) | data formatting | bytes 8388608 | tf_op jit(solution)/shard_map/convert_element_type | solution.py:48
  339.5 6.6 %copy.42 = bf16[128,8,2048]{2,0,1:T(8,128)(2,1)} copy(bf16[128,8,2048]{2,1,0:T(8,128)(2,1)} %convert_element_type.37) | data formatting | bytes 8388608 | tf_op jit(solution)/shard_map/convert_element_type | solution.py:48
  346.2 0.0 copy-start.1
  346.2 5.3 %all-to-all-start = ((bf16[128,8,2048]{2,0,1:T(8,128)(2,1)}), bf16[128,8,2048]{2,0,1:T(8,128)(2,1)}, u32[]{:S(2)}, u32[]{:S(2)}) async-start(bf16[128,8,2048]{2,0,1:T(8,128)(2,1)} %copy.42), calls=%async_computation | async-start | bytes 8388608 | tf_op jit(solution)/shard_map/all_to_all | solution.py:49
  351.4 0.0 copy-done.1
  351.4 1.3 copy.46
  352.7 89.4 %all-to-all-done = bf16[128,8,2048]{2,0,1:T(8,128)(2,1)} async-done(((bf16[128,8,2048]{2,0,1:T(8,128)(2,1)}), bf16[128,8,2048]{2,0,1:T(8,128)(2,1)}, u32[]{:S(2)}, u32[]{:S(2)}) %all-to-all-start) | async-done | bytes 4194336 | tf_op jit(solution)/shard_map/all_to_all | solution.py:49
  442.2 3.8 reduce_sum.12
  446.0 0.0 reduce-scatter.2.cloned.1.call-done
  446.0 9.1 %copy.47 = bf16[32,16,32,128]{3,2,1,0:T(8,128)(2,1)} copy(bf16[32,16,32,128]{3,1,0,2:T(8,128)(2,1)} %reduce-scatter.2.cloned.1.call-done) | data formatting | bytes 8388608
  (2 shorter events, 0.0 us)
Async XLA Ops:
  7.2 3.0 copy-start.2
  7.2 3.2 copy-start
  7.2 49.9 %all-gather.3.cloned.1.call-start = ((), (), s32[]{:S(2)}) async-start(), calls=%async_computation.2 | async-start | bytes 4718592 | tf_op jit(solution)/shard_map/all_gather | solution.py:17
  9.4 206.9 %all-gather.5.cloned.1.call-start = ((), (), s32[]{:S(2)}) async-start(), calls=%async_computation.3 | async-start | bytes 20971520 | tf_op jit(solution)/shard_map/all_gather | solution.py:23
  10.1 435.9 %reduce-scatter.2.cloned.1.call-start = ((), (), s32[]{:S(2)}) async-start(), calls=%async_computation.4 | async-start | bytes 20971520 | tf_op jit(solution)/shard_map/reduce_scatter | solution.py:33
  346.2 5.3 %copy-start.1 = (bf16[128,32,128]{0,2,1:T(8,128)(2,1)S(1)}, bf16[128,32,128]{0,2,1:T(8,128)(2,1)}, u32[]{:S(2)}) copy-start(bf16[128,32,128]{0,2,1:T(8,128)(2,1)} %get-tuple-element.16) | copy-start | bytes 3145732
  346.2 96.0 %all-to-all-start = ((bf16[128,8,2048]{2,0,1:T(8,128)(2,1)}), bf16[128,8,2048]{2,0,1:T(8,128)(2,1)}, u32[]{:S(2)}, u32[]{:S(2)}) async-start(bf16[128,8,2048]{2,0,1:T(8,128)(2,1)} %copy.42), calls=%async_computation | async-start | bytes 8388608 | tf_op jit(solution)/shard_map/all_to_all | solution.py:49
Sparse Core Ops, SparseCore 0:
  10.2 46.8 all-gather.2
  58.9 157.3 all-gather.4
  267.9 153.7 reduce-scatter.1
where the time goes:
time: 467 us; the launch traced here: 462 us
  waiting for transfers between devices  273 us (58%)
  matrix products  93.3 us (20%)
  local copies, waits for them, and re-layouts  72.3 us (15%)
  between operations  13.8 us (3%)
  starting transfers between devices  5.37 us (1%)
    all_gather x1, waiting for transfers between devices, on_device(): full_weight = lax.all_gather(weight, 'dp', axis=2, tiled=True)  137 us
    all_to_all x1, waiting for transfers between devices, on_device(): lax.all_to_all(outgoing, 'feat', split_axis=1, concat_axis=0, tiled=True)  89.4 us
    all_gather x1, waiting for transfers between devices, on_device(): gathered = lax.all_gather(tokens, 'feat', axis=1, tiled=True)  46.2 us
    dot_general x1, matrix products, on_device(): jnp.einsum('tqk,qb->tbk', partial_grad.reshape(tok_rows, local_rows * slo...  41.9 us
    convert_element_type x1, local copies, waits for them, and re-layouts, on_device(): weight_terms.astype(jnp.bfloat16)  22.5 us
    dot_general x1, matrix products, on_device(): jnp.einsum('tru,rsuk->trsk', grad_pre, full_weight, preferred_element_typ...  22.5 us
    gather x1, local copies, waits for them, and re-layouts, on_device(): gathered.reshape(tok_rows, block_count, side)[:, flat_cols, :]  16.2 us
    dot_general x1, matrix products, on_device(): jnp.einsum('tru,trsk->rsuk', grad_pre, picked, preferred_element_type=jnp...  14.9 us
  transfers between devices with their start and end apart: 4, of which 3 were waited for; matrix products, arithmetic and copies ran while one was open for 23% of the time, Pallas kernels for 0%

commit v1 on v0

--- a/solution.py
+++ b/solution.py
@@ -1,7 +1,14 @@
+import functools
+
 import jax
 import jax.numpy as jnp
 from jax import lax
+from jax.experimental import pallas as pl
+from jax.experimental.pallas import tpu as pltpu
 from jax.sharding import PartitionSpec as P
+
+MESH = pl.DeviceIdType.MESH
+LINE = 4
 
 
 def gelu_tanh(value):
@@ -53,9 +60,449 @@
     return (hidden, input_grad, weight_grad)
 
 
+def place():
+    i, f = lax.axis_index("dp"), lax.axis_index("feat")
+    z, c = f // 2, f % 2
+    px = i + 1 - 2 * (i % 2)
+    py = i + 2 - 4 * (i // 2)
+    return i, f, z, c, px, py, 3 - i
+
+
+def line_order(z):
+    m = z // 2
+    zz = z + m * (3 - 2 * z)
+    near = [zz, 1 - zz, 2 + 0 * zz, 3 + 0 * zz]
+    return [q + m * (3 - 2 * q) for q in near]
+
+
+def enter(i, f, z, px, py, pd):
+    barrier = pltpu.get_barrier_semaphore()
+
+    def greet(**where):
+        pl.semaphore_signal(barrier, inc=1, device_id=where, device_id_type=MESH)
+
+    for p in (px, py, pd):
+        greet(dp=p, feat=f)
+    greet(dp=i, feat=f + 1 - 2 * (f % 2))
+
+    @pl.when(z > 0)
+    def _():
+        greet(dp=i, feat=f - 2)
+
+    @pl.when(z < LINE - 1)
+    def _():
+        greet(dp=i, feat=f + 2)
+
+    pl.semaphore_wait(barrier, 5 + z * (LINE - 1 - z) // (LINE - 2))
+
+
+def rcopy(src, dst, send, recv, **where):
+    return pltpu.make_async_remote_copy(
+        src_ref=src, dst_ref=dst, send_sem=send, recv_sem=recv, device_id=where, device_id_type=MESH
+    )
+
+
+def gather_kernel(
+    tokens, cot, tok_all, cot_all, own, a2a_s, a2a_r, up_s, dn_s, line_r, xy_s, xy_r, dg_s, dg_r,
+    sib_s, sib_r,
+):
+    i, f, z, c, px, py, pd = place()
+    half = tokens.shape[0] // 2
+    order = line_order(z)
+    sib = f + 1 - 2 * c
+    enter(i, f, z, px, py, pd)
+
+    mine = pltpu.make_async_copy(tokens, tok_all.at[i, f], own.at[0])
+    mine.start()
+    keep = pltpu.make_async_copy(cot.at[i], cot_all.at[i], own.at[1])
+    keep.start()
+
+    def blk(who, zp):
+        return tok_all.at[who, 2 * zp + c]
+
+    def src(k):
+        return tokens if k == 0 else blk(i, order[k])
+
+    def up(k):
+        return rcopy(src(k), blk(i, order[k]), up_s.at[k], line_r.at[order[k]], dp=i, feat=f + 2)
+
+    def down(k):
+        return rcopy(src(k), blk(i, order[k]), dn_s.at[k], line_r.at[order[k]], dp=i, feat=f - 2)
+
+    def across(k, n):
+        return rcopy(
+            src(k), blk(i, order[k]), xy_s.at[n, k], xy_r.at[n, k], dp=(px, py)[n], feat=f
+        )
+
+    def corner(k, n):
+        rows = pl.ds(n * half, half)
+        ref = blk((px, py)[n], order[k]).at[rows]
+        return rcopy(ref, ref, dg_s.at[n, k], dg_r.at[n, k], dp=(py, px)[n], feat=f)
+
+    def twin(k, w):
+        who = (i, px, py, pd)[w]
+        ref = blk(who, order[k])
+        s = src(k) if w == 0 else ref
+        return rcopy(s, ref, sib_s.at[w, k], sib_r.at[w, k], dp=i, feat=sib)
+
+    def exchange(n):
+        p = (px, py, pd)[n]
+        return rcopy(cot.at[p], cot_all.at[i], a2a_s.at[n], a2a_r.at[n], dp=p, feat=f)
+
+    def goes_up(k):
+        return jnp.logical_and(order[k] <= z, z < LINE - 1)
+
+    def goes_down(k):
+        return jnp.logical_and(order[k] >= z, z > 0)
+
+    for k in range(LINE + 2):
+        if k < LINE:
+            if k > 0:
+                pltpu.make_async_copy(
+                    blk(i, order[k]), blk(i, order[k]), line_r.at[order[k]]
+                ).wait()
+            pl.when(goes_up(k))(lambda: up(k).start())
+            pl.when(goes_down(k))(lambda: down(k).start())
+            for n in range(2):
+                across(k, n).start()
+            twin(k, 0).start()
+        if 1 <= k <= LINE:
+            for n in range(2):
+                across(k - 1, n).wait_recv()
+                corner(k - 1, n).start()
+                twin(k - 1, 1 + n).start()
+        if k >= 2:
+            for n in range(2):
+                corner(k - 2, n).wait_recv()
+            twin(k - 2, 3).start()
+        if k == 1:
+            for n in range(3):
+                exchange(n).start()
+
+    for n in range(3):
+        exchange(n).wait()
+    mine.wait()
+    keep.wait()
+    for k in range(LINE):
+        pl.when(goes_up(k))(lambda: up(k).wait_send())
+        pl.when(goes_down(k))(lambda: down(k).wait_send())
+        for n in range(2):
+            across(k, n).wait_send()
+            corner(k, n).wait_send()
+        for w in range(4):
+            twin(k, w).wait()
+
+
+def spread_kernel(inv, weight, wd):
+    f = pl.program_id(0)
+    rows, slots, units, side = weight.shape
+    per = wd.shape[2] // side
+
+    def row(r, carry):
+        for b in range(per):
+            s = inv[r, f * per + b]
+            val = weight[r, jnp.minimum(s, slots - 1)]
+            val = jnp.where(s < slots, val, jnp.zeros_like(val))
+            wd[0, pl.ds(pl.multiple_of(r * units, units), units), b * side : (b + 1) * side] = val
+        return carry
+
+    lax.fori_loop(0, rows, row, 0)
+
+
+def local_kernel(cols, tok, weight, cot, hid, wgrad, grad_t, picked):
+    step = pl.program_id(0)
+    n, slots, units, side = weight.shape
+    groups, _, rows, wide = tok.shape
+    per = wide // side
+    grads = []
+    for a in range(n):
+        for s in range(slots):
+            b = cols[step * n + a, s]
+            lanes = pl.ds(pl.multiple_of((b % per) * side, side), side)
+            for g in range(groups):
+                picked[a % 2, g * rows : (g + 1) * rows, s * side : (s + 1) * side] = tok[
+                    g, b // per, :, lanes
+                ]
+        w = jnp.concatenate([weight[a, s] for s in range(slots)], axis=1)
+        x = picked.at[a % 2]
+        v = lax.dot_general(w, x[...], (((1,), (1,)), ((), ())), preferred_element_type=jnp.float32)
+        k0, k1 = 0.7978845608028654, 0.044715
+        th = jnp.tanh(k0 * (v + k1 * v * v * v))
+        act = (0.5 * v * (1.0 + th)).astype(jnp.bfloat16)
+        slope = 0.5 * (1.0 + th) + 0.5 * v * (1.0 - th * th) * (k0 * (1.0 + 3.0 * k1 * v * v))
+        ct = jnp.concatenate([cot[g, a] for g in range(groups)], axis=1).astype(jnp.float32)
+        grad = ct * slope
+        grads.append(grad)
+        grad = grad.astype(jnp.bfloat16)
+        for g in range(groups):
+            hid[g, a] = act[:, g * rows : (g + 1) * rows]
+        wg = jnp.dot(grad, x[...], preferred_element_type=jnp.float32).astype(jnp.bfloat16)
+        for s in range(slots):
+            wgrad[a, s] = wg[:, s * side : (s + 1) * side]
+    grad_t[...] = jnp.concatenate(grads, axis=0).T.astype(jnp.bfloat16)
+
+
+def scatter_kernel(
+    grad_t, wd, hid, out, hid_all, wbuf, part, sibbuf, xhalf, yhalf, xfull, yfull, upbuf, dnbuf,
+    own, wsem, a2a_s, a2a_r, sib_s, sib_r, half_s, half_r, full_s, full_r, up_s, up_r, dn_s, dn_r,
+):
+    i, f, z, c, px, py, pd = place()
+    groups, rows, wide = sibbuf.shape[1:]
+    half = rows // 2
+    order = line_order(z)[::-1]
+    sib = f + 1 - 2 * c
+    tile = 256
+
+    def fetch(q):
+        k, own_side = q // 2, q % 2
+        col = 2 * order[k] + (c if own_side else 1 - c)
+        return pltpu.make_async_copy(wd.at[col], wbuf.at[q % 2], wsem.at[q % 2])
+
+    fetch(0).start()
+    enter(i, f, z, px, py, pd)
+    keep = pltpu.make_async_copy(hid.at[i], hid_all.at[i], own)
+    keep.start()
+
+    def exchange(n):
+        p = (px, py, pd)[n]
+        return rcopy(hid.at[p], hid_all.at[i], a2a_s.at[n], a2a_r.at[n], dp=p, feat=f)
+
+    def work(q):
+        k = q // 2
+        fetch(q).wait()
+        if q + 1 < 2 * LINE:
+            fetch(q + 1).start()
+
+        def body(n, carry):
+            lanes = pl.ds(pl.multiple_of(n * tile, tile), tile)
+            res = jnp.dot(
+                grad_t[...], wbuf[q % 2, :, lanes], preferred_element_type=jnp.float32
+            ).astype(jnp.bfloat16)
+            for g in range(groups):
+                part[q % 2, k, g, :, lanes] = res[g * rows : (g + 1) * rows]
+            return carry
+
+        lax.fori_loop(0, wide // tile, body, 0)
+
+    def add(dst, *others):
+        def body(n, carry):
+            at = pl.ds(pl.multiple_of(n * 16, 16), 16)
+            total = dst[at].astype(jnp.float32)
+            for o in others:
+                total = total + o[at].astype(jnp.float32)
+            dst[at] = total.astype(jnp.bfloat16)
+            return carry
+
+        lax.fori_loop(0, dst.shape[0] // 16, body, 0)
+
+    def twin(k):
+        return rcopy(part.at[0, k], sibbuf.at[k], sib_s.at[k], sib_r.at[k], dp=i, feat=sib)
+
+    first, second = pl.ds(0, half), pl.ds(half, half)
+
+    def corner(k, n):
+        rows_n = (first, second)[n]
+        return rcopy(
+            part.at[1, k, pd, rows_n], (xhalf, yhalf)[n].at[k], half_s.at[n, k], half_r.at[n, k],
+            dp=(px, py)[n], feat=f,
+        )
+
+    def across(k, n):
+        p = (px, py)[n]
+        return rcopy(
+            part.at[1, k, p], (xfull, yfull)[n].at[k], full_s.at[n, k], full_r.at[n, k],
+            dp=p, feat=f,
+        )
+
+    def up(k):
+        return rcopy(
+            part.at[1, k, i], upbuf.at[order[k]], up_s.at[k], up_r.at[order[k]], dp=i, feat=f + 2
+        )
+
+    def down(k):
+        return rcopy(
+            part.at[1, k, i], dnbuf.at[order[k]], dn_s.at[k], dn_r.at[order[k]], dp=i, feat=f - 2
+        )
+
+    def got(buf, sem, k):
+        ref = buf.at[order[k]]
+        pltpu.make_async_copy(ref, ref, sem.at[order[k]]).wait()
+
+    def from_below(k):
+        return jnp.logical_and(order[k] >= z, z > 0)
+
+    def from_above(k):
+        return jnp.logical_and(order[k] <= z, z < LINE - 1)
+
+    for step in range(LINE + 3):
+        k = step
+        if k < LINE:
+            work(2 * k)
+            twin(k).start()
+            work(2 * k + 1)
+            if k == 0:
+                for n in range(3):
+                    exchange(n).start()
+            twin(k).wait_recv()
+            for g in (pd, px, py, i):
+                add(part.at[1, k, g], sibbuf.at[k, g])
+                if g is pd:
+                    corner(k, 0).start()
+                    corner(k, 1).start()
+        k = step - 1
+        if 0 <= k < LINE:
+            corner(k, 0).wait_recv()
+            add(part.at[1, k, py, first], xhalf.at[k])
+            across(k, 1).start()
+            corner(k, 1).wait_recv()
+            add(part.at[1, k, px, second], yhalf.at[k])
+            across(k, 0).start()
+        k = step - 2
+        if 0 <= k < LINE:
+            across(k, 0).wait_recv()
+            across(k, 1).wait_recv()
+            add(part.at[1, k, i], xfull.at[k], yfull.at[k])
+        k = step - 3
+        if 0 <= k < LINE:
+            mine = part.at[1, k, i]
+
+            @pl.when(from_below(k))
+            def _():
+                got(upbuf, up_r, k)
+                add(mine, upbuf.at[order[k]])
+
+            @pl.when(from_above(k))
+            def _():
+                got(dnbuf, dn_r, k)
+                add(mine, dnbuf.at[order[k]])
+
+            if k < LINE - 1:
+                pl.when(order[k] > z)(lambda: up(k).start())
+                pl.when(order[k] < z)(lambda: down(k).start())
+
+    done = pltpu.make_async_copy(part.at[1, LINE - 1, i], out, wsem.at[0])
+    done.start()
+    for n in range(3):
+        exchange(n).wait()
+    keep.wait()
+    for k in range(LINE):
+        twin(k).wait_send()
+        for n in range(2):
+            corner(k, n).wait_send()
+            across(k, n).wait_send()
+        if k < LINE - 1:
+            pl.when(order[k] > z)(lambda: up(k).wait_send())
+            pl.when(order[k] < z)(lambda: down(k).wait_send())
+    done.wait()
+
+
+def token_plan(tokens, columns, weight, cotangent):
+    rows, wide = tokens.shape
+    local, slots, units, side = weight.shape
+    n_dp, n_feat = lax.axis_size("dp"), lax.axis_size("feat")
+    bf = jnp.bfloat16
+    dma = pltpu.SemaphoreType.DMA
+    anywhere = pl.BlockSpec(memory_space=pl.ANY)
+    inside = pl.BlockSpec(memory_space=pltpu.VMEM)
+    blocks = n_feat * wide // side
+    total = n_dp * rows
+
+    cot_t = cotangent.reshape(rows, local, n_dp, units).transpose(2, 1, 3, 0)
+    tok_all, cot_all = pl.pallas_call(
+        gather_kernel,
+        out_shape=(
+            jax.ShapeDtypeStruct((n_dp, n_feat, rows, wide), bf),
+            jax.ShapeDtypeStruct(cot_t.shape, bf),
+        ),
+        in_specs=[anywhere] * 2,
+        out_specs=(anywhere,) * 2,
+        scratch_shapes=[
+            dma((2,)), dma((3,)), dma((3,)), dma((LINE,)), dma((LINE,)), dma((LINE,)),
+            dma((2, LINE)), dma((2, LINE)), dma((2, LINE)), dma((2, LINE)),
+            dma((4, LINE)), dma((4, LINE)),
+        ],
+        compiler_params=pltpu.CompilerParams(collective_id=0, has_side_effects=True),
+        name="gather",
+    )(tokens, cot_t)
+
+    hit = columns[:, :, None] == jnp.arange(blocks, dtype=jnp.int32)
+    inv = jnp.min(jnp.where(hit, jnp.arange(slots, dtype=jnp.int32)[:, None], slots), axis=1)
+    dense = pl.pallas_call(
+        spread_kernel,
+        out_shape=jax.ShapeDtypeStruct((n_feat, local * units, wide), bf),
+        grid_spec=pltpu.PrefetchScalarGridSpec(
+            num_scalar_prefetch=1,
+            grid=(n_feat,),
+            in_specs=[inside],
+            out_specs=pl.BlockSpec((1, local * units, wide), lambda f, inv: (f, 0, 0)),
+        ),
+        compiler_params=pltpu.CompilerParams(vmem_limit_bytes=32 * 2**20),
+        name="spread",
+    )(inv, weight)
+
+    n = side // units
+    hid_t, weight_grad, grad_t = pl.pallas_call(
+        local_kernel,
+        out_shape=(
+            jax.ShapeDtypeStruct(cot_t.shape, bf),
+            jax.ShapeDtypeStruct(weight.shape, bf),
+            jax.ShapeDtypeStruct((total, local * units), bf),
+        ),
+        grid_spec=pltpu.PrefetchScalarGridSpec(
+            num_scalar_prefetch=1,
+            grid=(local // n,),
+            in_specs=[
+                inside,
+                pl.BlockSpec((n, slots, units, side), lambda r, c: (r, 0, 0, 0)),
+                pl.BlockSpec((n_dp, n, units, rows), lambda r, c: (0, r, 0, 0)),
+            ],
+            out_specs=(
+                pl.BlockSpec((n_dp, n, units, rows), lambda r, c: (0, r, 0, 0)),
+                pl.BlockSpec((n, slots, units, side), lambda r, c: (r, 0, 0, 0)),
+                pl.BlockSpec((total, n * units), lambda r, c: (0, r)),
+            ),
+            scratch_shapes=[pltpu.VMEM((2, total, slots * side), bf)],
+        ),
+        compiler_params=pltpu.CompilerParams(vmem_limit_bytes=48 * 2**20),
+        name="local",
+    )(columns, tok_all, weight, cot_all)
+
+    input_grad, hid_all = pl.pallas_call(
+        scatter_kernel,
+        out_shape=(
+            jax.ShapeDtypeStruct((rows, wide), bf),
+            jax.ShapeDtypeStruct(cot_t.shape, bf),
+        ),
+        in_specs=[inside, anywhere, anywhere],
+        out_specs=(anywhere,) * 2,
+        scratch_shapes=[
+            pltpu.VMEM((2, local * units, wide), bf),
+            pltpu.VMEM((2, LINE, n_dp, rows, wide), bf),
+            pltpu.VMEM((LINE, n_dp, rows, wide), bf),
+            pltpu.VMEM((LINE, rows // 2, wide), bf),
+            pltpu.VMEM((LINE, rows // 2, wide), bf),
+            pltpu.VMEM((LINE, rows, wide), bf),
+            pltpu.VMEM((LINE, rows, wide), bf),
+            pltpu.VMEM((LINE, rows, wide), bf),
+            pltpu.VMEM((LINE, rows, wide), bf),
+            dma(()), dma((2,)), dma((3,)), dma((3,)), dma((LINE,)), dma((LINE,)),
+            dma((2, LINE)), dma((2, LINE)), dma((2, LINE)), dma((2, LINE)),
+            dma((LINE,)), dma((LINE,)), dma((LINE,)), dma((LINE,)),
+        ],
+        compiler_params=pltpu.CompilerParams(
+            collective_id=1, has_side_effects=True, vmem_limit_bytes=56 * 2**20
+        ),
+        name="scatter",
+    )(grad_t, dense, hid_t)
+    hidden = hid_all.transpose(3, 1, 0, 2).reshape(rows, local * side)
+    return (hidden, input_grad, weight_grad)
+
+
 def solution(mesh):
     in_specs = (P("dp", "feat"), P("feat", None), P("feat", None, "dp", None), P("dp", "feat"))
     out_specs = (P("dp", "feat"), P("dp", "feat"), P("feat", None, "dp", None))
+    square = mesh.shape["dp"] == 4 and mesh.shape["feat"] == 2 * LINE
     return jax.shard_map(
-        on_device, mesh=mesh, in_specs=in_specs, out_specs=out_specs, check_vma=False
-    )
+        token_plan if square else on_device,
+        mesh=mesh, in_specs=in_specs, out_specs=out_specs, check_vma=False,
+    )

time: 467 us -> 285 us (0.61)
  waiting for transfers between devices: 273 us -> 0 us
  Pallas kernels: 0 us -> 269 us
  matrix products: 93.3 us -> 0 us
  local copies, waits for them, and re-layouts: 72.3 us -> 11.3 us
  between operations: 13.8 us -> 0.69 us
  starting transfers between devices: 5.37 us -> 0 us
    pallas_call x0 -> x4, Pallas kernels: none -> 269 us  [the longest x1 106 us: token_plan(): pl.pallas_call(scatter_kernel, out_shape=(jax.ShapeDtypeStruct((rows, wid...]
    all_gather x2 -> x0, waiting for transfers between devices: 183 us -> none  [the longest x1 137 us: on_device(): full_weight = lax.all_gather(weight, 'dp', axis=2, tiled=True)]
    dot_general x4 -> x0, matrix products: 93.3 us -> none  [the longest x1 41.9 us: on_device(): jnp.einsum('tqk,qb->tbk', partial_grad.reshape(tok_rows, local_rows * slo...]
    all_to_all x1 -> x0, waiting for transfers between devices: 89.4 us -> none  [on_device(): lax.all_to_all(outgoing, 'feat', split_axis=1, concat_axis=0, tiled=True)]
    convert_element_type x4 -> x0, local copies, waits for them, and re-layouts: 37 us -> none  [the longest x1 22.5 us: on_device(): weight_terms.astype(jnp.bfloat16)]
    gather x1 -> x0, local copies, waits for them, and re-layouts: 16.2 us -> none  [on_device(): gathered.reshape(tok_rows, block_count, side)[:, flat_cols, :]]
    reshape x2 -> x1, local copies, waits for them, and re-layouts: 6.44 us -> 1.07 us  [token_plan(): cot_t = cotangent.reshape(rows, local, n_dp, units).transpose(2, 1, 3, 0)]
    all_to_all x1 -> x0, starting transfers between devices: 5.25 us -> none  [on_device(): lax.all_to_all(outgoing, 'feat', split_axis=1, concat_axis=0, tiled=True)]
  transfers between devices with their start and end apart: 4 -> 0, of which waited for: 3 -> 0; matrix products, arithmetic and copies ran while one was open for 23% -> 0% of each run, Pallas kernels for 0% -> 0%
where the time goes in v1:
time: 285 us; the launch traced here: 281 us
  Pallas kernels  269 us (94%)
  local copies, waits for them, and re-layouts  11.3 us (4%)
    pallas_call x1, Pallas kernels, token_plan(): pl.pallas_call(scatter_kernel, out_shape=(jax.ShapeDtypeStruct((rows, wid...  106 us
    pallas_call x1, Pallas kernels, token_plan(): pl.pallas_call(gather_kernel, out_shape=(jax.ShapeDtypeStruct((n_dp, n_fe...  86.8 us
    pallas_call x1, Pallas kernels, token_plan(): pl.pallas_call(local_kernel, out_shape=(jax.ShapeDtypeStruct(cot_t.shape,...  51.1 us
    pallas_call x1, Pallas kernels, token_plan(): pl.pallas_call(spread_kernel, out_shape=jax.ShapeDtypeStruct((n_feat, loc...  24.7 us
    unnamed x12, local copies, waits for them, and re-layouts  8.9 us

profile of v1, /device:TPU:18, one launch (start us, length us, event | category | flops | bytes accessed | tf_op | source)
XLA Modules:
  0.0 281.0 jit_solution(12450871436694016300)
XLA Ops:
  0.6 0.8 copy.17.cols
  1.4 0.2 select_reduce_fusion.inv
  1.6 1.6 copy.15
  3.2 1.1 copy.22
  4.3 86.8 %gather.1 = (bf16[4,8,128,2048]{3,2,1,0:T(8,128)(2,1)}, bf16[4,32,32,128]{3,2,1,0:T(8,128)(2,1)}) custom-call(bf16[128,2048]{1,0:T(8,128)(2,1)} %tokens.1, bf16[4,32,32,128]{3,2,1,0:T(8,128)(2,1)} %bitcast.6), custom_call_target="tpu_custom_call" | custom-call | tf_op jit(solution)/shard_map/gather/pallas_call | solution.py:411
  91.0 0.0 copy-start
  91.1 0.0 copy-start.3
  91.1 1.4 copy-done.3
  92.4 51.1 %local.1 = (bf16[4,32,32,128]{3,2,1,0:T(8,128)(2,1)S(1)}, bf16[32,16,32,128]{3,2,1,0:T(8,128)(2,1)}, bf16[512,1024]{1,0:T(8,128)(2,1)S(1)}) custom-call(s32[32,16]{1,0:T(8,128)S(1)} %copy.17.cols, bf16[4,8,128,2048]{3,2,1,0:T(8,128)(2,1)} %get-tuple-element.10.tok, bf16[32,16,32,128]{3,2,1,0:T(8,128)(2,1)} %weight.3, bf16[4,32,32,128]{3,2,1,0:T(8,128)(2,1)S(1)} %copy-done.3), custom_call_target="tpu_custom_call" | custom-call | tf_op jit(solution)/shard_map/local/pallas_call | solution.py:444
  143.5 0.0 copy-start.1
  143.5 1.0 copy-done.1
  144.5 0.0 copy-start.2
  144.5 1.0 copy-done.2
  145.4 0.0 copy-done
  145.4 24.7 %spread.1.wd = bf16[8,1024,2048]{2,1,0:T(8,128)(2,1)} custom-call(s32[32,128]{1,0:T(8,128)S(1)} %select_reduce_fusion.inv, bf16[32,16,32,128]{3,2,1,0:T(8,128)(2,1)S(1)} %copy-done), custom_call_target="tpu_custom_call" | custom-call | tf_op jit(solution)/shard_map/spread/pallas_call | solution.py:430
  170.1 106.3 %scatter.1 = (bf16[128,2048]{1,0:T(8,128)(2,1)}, bf16[4,32,32,128]{3,2,1,0:T(8,128)(2,1)}) custom-call(bf16[512,1024]{1,0:T(8,128)(2,1)} %copy-done.2, bf16[8,1024,2048]{2,1,0:T(8,128)(2,1)} %spread.1.wd, bf16[4,32,32,128]{3,2,1,0:T(8,128)(2,1)} %copy-done.1), custom_call_target="tpu_custom_call" | custom-call | tf_op jit(solution)/shard_map/scatter/pallas_call | solution.py:470
  276.4 1.4 copy.19
  277.8 1.3 copy.20
  279.1 1.9 copy.24
Async XLA Ops:
  91.0 54.4 %copy-start = (bf16[32,16,32,128]{3,2,1,0:T(8,128)(2,1)S(1)}, bf16[32,16,32,128]{3,2,1,0:T(8,128)(2,1)}, u32[]{:S(2)}) copy-start(bf16[32,16,32,128]{3,2,1,0:T(8,128)(2,1)} %weight.3) | copy-start | bytes 12582916
  91.1 1.4 copy-start.3
  143.5 1.0 copy-start.1
  144.5 1.0 copy-start.2

commit v2 on v1

--- a/solution.py
+++ b/solution.py
@@ -103,14 +103,54 @@
 
 
 def gather_kernel(
-    tokens, cot, tok_all, cot_all, own, a2a_s, a2a_r, up_s, dn_s, line_r, xy_s, xy_r, dg_s, dg_r,
-    sib_s, sib_r,
+    tokens, cot, inv, weight, tok_all, cot_all, dense, pre, filled, wd, chunk, own, wsem, csem,
+    a2a_s, a2a_r, up_s, dn_s, line_r, xy_s, xy_r, dg_s, dg_r, sib_s, sib_r,
 ):
     i, f, z, c, px, py, pd = place()
     half = tokens.shape[0] // 2
     order = line_order(z)
     sib = f + 1 - 2 * c
+    local, slots, units, side = weight.shape
+    per = wd.shape[2] // side
+    load = pltpu.make_async_copy(weight, filled.at[:, pl.ds(0, slots)], own.at[2])
+    load.start()
+    filled[:, slots] = jnp.zeros((local, units, side), filled.dtype)
     enter(i, f, z, px, py, pd)
+
+    def owner(q):
+        return 2 * order[q // 2] + (c if q % 2 == 0 else 1 - c)
+
+    def keep_dense(q):
+        return pltpu.make_async_copy(wd.at[q], dense.at[owner(q)], wsem.at[q])
+
+    def build(q):
+        first = owner(q) * per
+
+        def row(r, carry):
+            at = pl.ds(pl.multiple_of(r * units, units), units)
+            for b in range(per):
+                wd[q, at, b * side : (b + 1) * side] = filled[r, inv[r, first + b]]
+            return carry
+
+        lax.fori_loop(0, local, row, 0)
+        keep_dense(q).start()
+
+    def forward(q):
+        fetch = pltpu.make_async_copy(tok_all.at[:, owner(q)], chunk, csem)
+        fetch.start()
+        fetch.wait()
+        pair = 2 * chunk.shape[1]
+
+        def body(n, carry):
+            lanes = pl.ds(pl.multiple_of(n * pair, pair), pair)
+            x = chunk[pl.ds(2 * n, 2)].reshape(pair, chunk.shape[2])
+            res = lax.dot_general(
+                wd[q], x, (((1,), (1,)), ((), ())), preferred_element_type=jnp.float32
+            )
+            pre[:, lanes] = res if q == 0 else pre[:, lanes] + res
+            return carry
+
+        lax.fori_loop(0, chunk.shape[0] // 2, body, 0)
 
     mine = pltpu.make_async_copy(tokens, tok_all.at[i, f], own.at[0])
     mine.start()
@@ -155,7 +195,8 @@
     def goes_down(k):
         return jnp.logical_and(order[k] >= z, z > 0)
 
-    for k in range(LINE + 2):
+    builds = ((0, 1, 2), (3, 4, 5), (6, 7))
+    for k in range(LINE + 3):
         if k < LINE:
             if k > 0:
                 pltpu.make_async_copy(
@@ -171,17 +212,31 @@
                 across(k - 1, n).wait_recv()
                 corner(k - 1, n).start()
                 twin(k - 1, 1 + n).start()
-        if k >= 2:
+        if 2 <= k < LINE + 2:
             for n in range(2):
                 corner(k - 2, n).wait_recv()
             twin(k - 2, 3).start()
         if k == 1:
             for n in range(3):
                 exchange(n).start()
+        if k == 0:
+            load.wait()
+        if k < len(builds):
+            for q in builds[k]:
+                build(q)
+        if k == 2:
+            mine.wait()
+        if 2 <= k < LINE + 2:
+            forward(2 * (k - 2))
+        if k >= 3:
+            for w in range(4):
+                twin(k - 3, w).wait_recv()
+            forward(2 * (k - 3) + 1)
 
     for n in range(3):
         exchange(n).wait()
-    mine.wait()
+    for q in range(2 * LINE):
+        keep_dense(q).wait()
     keep.wait()
     for k in range(LINE):
         pl.when(goes_up(k))(lambda: up(k).wait_send())
@@ -190,28 +245,12 @@
             across(k, n).wait_send()
             corner(k, n).wait_send()
         for w in range(4):
-            twin(k, w).wait()
-
-
-def spread_kernel(inv, weight, wd):
-    f = pl.program_id(0)
-    rows, slots, units, side = weight.shape
-    per = wd.shape[2] // side
-
-    def row(r, carry):
-        for b in range(per):
-            s = inv[r, f * per + b]
-            val = weight[r, jnp.minimum(s, slots - 1)]
-            val = jnp.where(s < slots, val, jnp.zeros_like(val))
-            wd[0, pl.ds(pl.multiple_of(r * units, units), units), b * side : (b + 1) * side] = val
-        return carry
-
-    lax.fori_loop(0, rows, row, 0)
-
-
-def local_kernel(cols, tok, weight, cot, hid, wgrad, grad_t, picked):
+            twin(k, w).wait_send()
+
+
+def local_kernel(cols, tok, pre, cot, hid, wgrad, grad_t, picked):
     step = pl.program_id(0)
-    n, slots, units, side = weight.shape
+    n, slots, units, side = wgrad.shape
     groups, _, rows, wide = tok.shape
     per = wide // side
     grads = []
@@ -223,9 +262,8 @@
                 picked[a % 2, g * rows : (g + 1) * rows, s * side : (s + 1) * side] = tok[
                     g, b // per, :, lanes
                 ]
-        w = jnp.concatenate([weight[a, s] for s in range(slots)], axis=1)
         x = picked.at[a % 2]
-        v = lax.dot_general(w, x[...], (((1,), (1,)), ((), ())), preferred_element_type=jnp.float32)
+        v = pre[a * units : (a + 1) * units, :]
         k0, k1 = 0.7978845608028654, 0.044715
         th = jnp.tanh(k0 * (v + k1 * v * v * v))
         act = (0.5 * v * (1.0 + th)).astype(jnp.bfloat16)
@@ -408,37 +446,32 @@
     total = n_dp * rows
 
     cot_t = cotangent.reshape(rows, local, n_dp, units).transpose(2, 1, 3, 0)
-    tok_all, cot_all = pl.pallas_call(
+    hit = columns[:, :, None] == jnp.arange(blocks, dtype=jnp.int32)
+    inv = jnp.min(jnp.where(hit, jnp.arange(slots, dtype=jnp.int32)[:, None], slots), axis=1)
+    tok_all, cot_all, dense, pre = pl.pallas_call(
         gather_kernel,
         out_shape=(
             jax.ShapeDtypeStruct((n_dp, n_feat, rows, wide), bf),
             jax.ShapeDtypeStruct(cot_t.shape, bf),
+            jax.ShapeDtypeStruct((n_feat, local * units, wide), bf),
+            jax.ShapeDtypeStruct((local * units, total), jnp.float32),
         ),
-        in_specs=[anywhere] * 2,
-        out_specs=(anywhere,) * 2,
+        in_specs=[anywhere, anywhere, pl.BlockSpec(memory_space=pltpu.SMEM), anywhere],
+        out_specs=(anywhere, anywhere, anywhere, inside),
         scratch_shapes=[
-            dma((2,)), dma((3,)), dma((3,)), dma((LINE,)), dma((LINE,)), dma((LINE,)),
+            pltpu.VMEM((local, slots + 1, units, side), bf),
+            pltpu.VMEM((n_feat, local * units, wide), bf),
+            pltpu.VMEM((n_dp, rows, wide), bf),
+            dma((3,)), dma((n_feat,)), dma(()),
+            dma((3,)), dma((3,)), dma((LINE,)), dma((LINE,)), dma((LINE,)),
             dma((2, LINE)), dma((2, LINE)), dma((2, LINE)), dma((2, LINE)),
             dma((4, LINE)), dma((4, LINE)),
         ],
-        compiler_params=pltpu.CompilerParams(collective_id=0, has_side_effects=True),
+        compiler_params=pltpu.CompilerParams(
+            collective_id=0, has_side_effects=True, vmem_limit_bytes=56 * 2**20
+        ),
         name="gather",
-    )(tokens, cot_t)
-
-    hit = columns[:, :, None] == jnp.arange(blocks, dtype=jnp.int32)
-    inv = jnp.min(jnp.where(hit, jnp.arange(slots, dtype=jnp.int32)[:, None], slots), axis=1)
-    dense = pl.pallas_call(
-        spread_kernel,
-        out_shape=jax.ShapeDtypeStruct((n_feat, local * units, wide), bf),
-        grid_spec=pltpu.PrefetchScalarGridSpec(
-            num_scalar_prefetch=1,
-            grid=(n_feat,),
-            in_specs=[inside],
-            out_specs=pl.BlockSpec((1, local * units, wide), lambda f, inv: (f, 0, 0)),
-        ),
-        compiler_params=pltpu.CompilerParams(vmem_limit_bytes=32 * 2**20),
-        name="spread",
-    )(inv, weight)
+    )(tokens, cot_t, inv, weight)
 
     n = side // units
     hid_t, weight_grad, grad_t = pl.pallas_call(
@@ -453,7 +486,7 @@
             grid=(local // n,),
             in_specs=[
                 inside,
-                pl.BlockSpec((n, slots, units, side), lambda r, c: (r, 0, 0, 0)),
+                pl.BlockSpec((n * units, total), lambda r, c: (r, 0)),
                 pl.BlockSpec((n_dp, n, units, rows), lambda r, c: (0, r, 0, 0)),
             ],
             out_specs=(
@@ -465,7 +498,7 @@
         ),
         compiler_params=pltpu.CompilerParams(vmem_limit_bytes=48 * 2**20),
         name="local",
-    )(columns, tok_all, weight, cot_all)
+    )(columns, tok_all, pre, cot_all)
 
     input_grad, hid_all = pl.pallas_call(
         scatter_kernel,

time: 285 us -> 260 us (0.912)
  Pallas kernels: 269 us -> 244 us
    pallas_call x1 -> x0, Pallas kernels: 24.7 us -> none  [token_plan(): pl.pallas_call(spread_kernel, out_shape=jax.ShapeDtypeStruct((n_feat, loc...]
    pallas_call x1, Pallas kernels: 86.8 us -> 104 us  [token_plan(): pl.pallas_call(gather_kernel, out_shape=(jax.ShapeDtypeStruct((n_dp, n_fe...]
    pallas_call x1, Pallas kernels: 51.1 us -> 38.5 us  [token_plan(): pl.pallas_call(local_kernel, out_shape=(jax.ShapeDtypeStruct(cot_t.shape,...]
    pallas_call x1, Pallas kernels: 106 us -> 101 us  [token_plan(): pl.pallas_call(scatter_kernel, out_shape=(jax.ShapeDtypeStruct((rows, wid...]
    unnamed x12 -> x14, local copies, waits for them, and re-layouts: 8.9 us -> 9.24 us
where the time goes in v2:
time: 260 us; the launch traced here: 257 us
  Pallas kernels  244 us (94%)
  local copies, waits for them, and re-layouts  11.7 us (4%)
    pallas_call x1, Pallas kernels, token_plan(): pl.pallas_call(gather_kernel, out_shape=(jax.ShapeDtypeStruct((n_dp, n_fe...  104 us
    pallas_call x1, Pallas kernels, token_plan(): pl.pallas_call(scatter_kernel, out_shape=(jax.ShapeDtypeStruct((rows, wid...  101 us
    pallas_call x1, Pallas kernels, token_plan(): pl.pallas_call(local_kernel, out_shape=(jax.ShapeDtypeStruct(cot_t.shape,...  38.5 us
    unnamed x14, local copies, waits for them, and re-layouts  9.24 us

profile of v2, /device:TPU:18, one launch (start us, length us, event | category | flops | bytes accessed | tf_op | source)
XLA Modules:
  0.0 257.5 jit_solution(13038825499424926135)
XLA Ops:
  0.6 0.8 copy.18.cols
  1.4 0.8 select_reduce_fusion.inv
  2.2 1.6 copy.15
  3.8 1.1 copy.22
  4.9 104.4 %gather.1 = (bf16[4,8,128,2048]{3,2,1,0:T(8,128)(2,1)}, bf16[4,32,32,128]{3,2,1,0:T(8,128)(2,1)}, bf16[8,1024,2048]{2,1,0:T(8,128)(2,1)}, f32[1024,512]{1,0:T(8,128)}) custom-call(bf16[128,2048]{1,0:T(8,128)(2,1)} %tokens.1, bf16[4,32,32,128]{3,2,1,0:T(8,128)(2,1)} %bitcast.8, s32[32,128]{1,0:T(8,128)} %select_reduce_fusion.inv, bf16[32,16,32,128]{3,2,1,0:T(8,128)(2,1)} %weight.1), custom_call_target="tpu_custom_call" | custom-call | tf_op jit(solution)/shard_map/gather/pallas_call | solution.py:451
  109.3 0.0 copy-start
  109.3 1.6 copy-done
  110.9 0.0 copy-start.1
  110.9 1.2 copy-done.1
  112.1 38.5 %local.1 = (bf16[4,32,32,128]{3,2,1,0:T(8,128)(2,1)S(1)}, bf16[32,16,32,128]{3,2,1,0:T(8,128)(2,1)}, bf16[512,1024]{1,0:T(8,128)(2,1)S(1)}) custom-call(s32[32,16]{1,0:T(8,128)S(1)} %copy.18.cols, bf16[4,8,128,2048]{3,2,1,0:T(8,128)(2,1)} %get-tuple-element.12.tok, f32[1024,512]{1,0:T(8,128)S(1)} %copy-done, bf16[4,32,32,128]{3,2,1,0:T(8,128)(2,1)S(1)} %copy-done.1), custom_call_target="tpu_custom_call" | custom-call | tf_op jit(solution)/shard_map/local/pallas_call | solution.py:477
  150.6 0.0 copy-start.2
  150.6 1.0 copy-done.2
  151.6 0.0 copy-start.3
  151.6 1.0 copy-done.3
  152.6 101.4 %scatter.1 = (bf16[128,2048]{1,0:T(8,128)(2,1)}, bf16[4,32,32,128]{3,2,1,0:T(8,128)(2,1)}) custom-call(bf16[512,1024]{1,0:T(8,128)(2,1)} %copy-done.3, bf16[8,1024,2048]{2,1,0:T(8,128)(2,1)} %get-tuple-element.16.wd, bf16[4,32,32,128]{3,2,1,0:T(8,128)(2,1)} %copy-done.2), custom_call_target="tpu_custom_call" | custom-call | tf_op jit(solution)/shard_map/scatter/pallas_call | solution.py:503
  253.9 0.0 copy-start.4
  254.0 1.4 copy.19
  255.4 1.3 copy.20
  256.7 0.0 copy-done.4
  256.7 0.8 copy.24
Async XLA Ops:
  109.3 1.6 copy-start
  110.9 1.2 copy-start.1
  150.6 1.0 copy-start.2
  151.6 1.0 copy-start.3
  253.9 2.7 %copy-start.4 = (bf16[128,2048]{1,0:T(8,128)(2,1)S(1)}, bf16[128,2048]{1,0:T(8,128)(2,1)}, u32[]{:S(2)}) copy-start(bf16[128,2048]{1,0:T(8,128)(2,1)} %get-tuple-element.31) | copy-start | bytes 1572868

commit v3 on v2

--- a/solution.py
+++ b/solution.py
@@ -104,7 +104,7 @@
 
 def gather_kernel(
     tokens, cot, inv, weight, tok_all, cot_all, dense, pre, filled, wd, chunk, own, wsem, csem,
-    a2a_s, a2a_r, up_s, dn_s, line_r, xy_s, xy_r, dg_s, dg_r, sib_s, sib_r,
+    a2a_s, a2a_r, up_s, dn_s, line_r, up2_s, dn2_s, line2_r, xy_s, xy_r, dg_s, dg_r, sib_s, sib_r,
 ):
     i, f, z, c, px, py, pd = place()
     half = tokens.shape[0] // 2
@@ -169,6 +169,14 @@
     def down(k):
         return rcopy(src(k), blk(i, order[k]), dn_s.at[k], line_r.at[order[k]], dp=i, feat=f - 2)
 
+    def up2(k):
+        ref = blk(pd, order[k])
+        return rcopy(ref, ref, up2_s.at[k], line2_r.at[order[k]], dp=i, feat=f + 2)
+
+    def down2(k):
+        ref = blk(pd, order[k])
+        return rcopy(ref, ref, dn2_s.at[k], line2_r.at[order[k]], dp=i, feat=f - 2)
+
     def across(k, n):
         return rcopy(
             src(k), blk(i, order[k]), xy_s.at[n, k], xy_r.at[n, k], dp=(px, py)[n], feat=f
@@ -177,7 +185,7 @@
     def corner(k, n):
         rows = pl.ds(n * half, half)
         ref = blk((px, py)[n], order[k]).at[rows]
-        return rcopy(ref, ref, dg_s.at[n, k], dg_r.at[n, k], dp=(py, px)[n], feat=f)
+        return rcopy(ref, ref, dg_s.at[n], dg_r.at[n], dp=(py, px)[n], feat=f)
 
     def twin(k, w):
         who = (i, px, py, pd)[w]
@@ -210,11 +218,18 @@
         if 1 <= k <= LINE:
             for n in range(2):
                 across(k - 1, n).wait_recv()
-                corner(k - 1, n).start()
+                if k == 1:
+                    corner(0, n).start()
                 twin(k - 1, 1 + n).start()
         if 2 <= k < LINE + 2:
-            for n in range(2):
-                corner(k - 2, n).wait_recv()
+            if k == 2:
+                for n in range(2):
+                    corner(0, n).wait_recv()
+            else:
+                ref = blk(pd, order[k - 2])
+                pltpu.make_async_copy(ref, ref, line2_r.at[order[k - 2]]).wait()
+            pl.when(goes_up(k - 2))(lambda: up2(k - 2).start())
+            pl.when(goes_down(k - 2))(lambda: down2(k - 2).start())
             twin(k - 2, 3).start()
         if k == 1:
             for n in range(3):
@@ -241,9 +256,12 @@
     for k in range(LINE):
         pl.when(goes_up(k))(lambda: up(k).wait_send())
         pl.when(goes_down(k))(lambda: down(k).wait_send())
+        pl.when(goes_up(k))(lambda: up2(k).wait_send())
+        pl.when(goes_down(k))(lambda: down2(k).wait_send())
         for n in range(2):
             across(k, n).wait_send()
-            corner(k, n).wait_send()
+            if k == 0:
+                corner(k, n).wait_send()
         for w in range(4):
             twin(k, w).wait_send()
 
@@ -282,7 +300,8 @@
 
 def scatter_kernel(
     grad_t, wd, hid, out, hid_all, wbuf, part, sibbuf, xhalf, yhalf, xfull, yfull, upbuf, dnbuf,
-    own, wsem, a2a_s, a2a_r, sib_s, sib_r, half_s, half_r, full_s, full_r, up_s, up_r, dn_s, dn_r,
+    up2buf, dn2buf, own, wsem, a2a_s, a2a_r, sib_s, sib_r, half_s, half_r, full_s, full_r, up_s, up_r, dn_s, dn_r,
+    up2_s, up2_r, dn2_s, dn2_r,
 ):
     i, f, z, c, px, py, pd = place()
     groups, rows, wide = sibbuf.shape[1:]
@@ -341,7 +360,7 @@
     def corner(k, n):
         rows_n = (first, second)[n]
         return rcopy(
-            part.at[1, k, pd, rows_n], (xhalf, yhalf)[n].at[k], half_s.at[n, k], half_r.at[n, k],
+            part.at[1, k, pd, rows_n], (xhalf, yhalf)[n], half_s.at[n], half_r.at[n],
             dp=(px, py)[n], feat=f,
         )
 
@@ -360,6 +379,16 @@
     def down(k):
         return rcopy(
             part.at[1, k, i], dnbuf.at[order[k]], dn_s.at[k], dn_r.at[order[k]], dp=i, feat=f - 2
+        )
+
+    def up2(k):
+        return rcopy(
+            part.at[1, k, pd], up2buf.at[order[k]], up2_s.at[k], up2_r.at[order[k]], dp=i, feat=f + 2
+        )
+
+    def down2(k):
+        return rcopy(
+            part.at[1, k, pd], dn2buf.at[order[k]], dn2_s.at[k], dn2_r.at[order[k]], dp=i, feat=f - 2
         )
 
     def got(buf, sem, k):
@@ -372,7 +401,19 @@
     def from_above(k):
         return jnp.logical_and(order[k] <= z, z < LINE - 1)
 
-    for step in range(LINE + 3):
+    def collect(k, mine, ups, downs):
+        @pl.when(from_below(k))
+        def _():
+            got(ups[0], ups[1], k)
+            add(mine, ups[0].at[order[k]])
+
+        @pl.when(from_above(k))
+        def _():
+            got(downs[0], downs[1], k)
+            add(mine, downs[0].at[order[k]])
+
+    last = LINE - 1
+    for step in range(LINE + 2):
         k = step
         if k < LINE:
             work(2 * k)
@@ -382,41 +423,40 @@
                 for n in range(3):
                     exchange(n).start()
             twin(k).wait_recv()
-            for g in (pd, px, py, i):
+            add(part.at[1, k, pd], sibbuf.at[k, pd])
+            for n, g in ((0, px), (1, py)):
                 add(part.at[1, k, g], sibbuf.at[k, g])
-                if g is pd:
-                    corner(k, 0).start()
-                    corner(k, 1).start()
+                if k < last:
+                    across(k, n).start()
+            add(part.at[1, k, i], sibbuf.at[k, i])
+            collect(k, part.at[1, k, pd], (up2buf, up2_r), (dn2buf, dn2_r))
+            if k < last:
+                pl.when(order[k] > z)(lambda: up2(k).start())
+                pl.when(order[k] < z)(lambda: down2(k).start())
+            else:
+                corner(k, 0).start()
+                corner(k, 1).start()
         k = step - 1
         if 0 <= k < LINE:
-            corner(k, 0).wait_recv()
-            add(part.at[1, k, py, first], xhalf.at[k])
-            across(k, 1).start()
-            corner(k, 1).wait_recv()
-            add(part.at[1, k, px, second], yhalf.at[k])
-            across(k, 0).start()
-        k = step - 2
-        if 0 <= k < LINE:
-            across(k, 0).wait_recv()
-            across(k, 1).wait_recv()
-            add(part.at[1, k, i], xfull.at[k], yfull.at[k])
-        k = step - 3
-        if 0 <= k < LINE:
-            mine = part.at[1, k, i]
-
-            @pl.when(from_below(k))
-            def _():
-                got(upbuf, up_r, k)
-                add(mine, upbuf.at[order[k]])
-
-            @pl.when(from_above(k))
-            def _():
-                got(dnbuf, dn_r, k)
-                add(mine, dnbuf.at[order[k]])
-
-            if k < LINE - 1:
+            if k == last:
+                corner(k, 0).wait_recv()
+                add(part.at[1, k, py, first], xhalf)
+                across(k, 1).start()
+                corner(k, 1).wait_recv()
+                add(part.at[1, k, px, second], yhalf)
+                across(k, 0).start()
+            else:
+                across(k, 0).wait_recv()
+                across(k, 1).wait_recv()
+                add(part.at[1, k, i], xfull.at[k], yfull.at[k])
+                collect(k, part.at[1, k, i], (upbuf, up_r), (dnbuf, dn_r))
                 pl.when(order[k] > z)(lambda: up(k).start())
                 pl.when(order[k] < z)(lambda: down(k).start())
+        if step == LINE + 1:
+            collect(last, part.at[1, last, i], (upbuf, up_r), (dnbuf, dn_r))
+            across(last, 0).wait_recv()
+            across(last, 1).wait_recv()
+            add(part.at[1, last, i], xfull.at[last], yfull.at[last])
 
     done = pltpu.make_async_copy(part.at[1, LINE - 1, i], out, wsem.at[0])
     done.start()
@@ -426,11 +466,14 @@
     for k in range(LINE):
         twin(k).wait_send()
         for n in range(2):
-            corner(k, n).wait_send()
+            if k == last:
+                corner(k, n).wait_send()
             across(k, n).wait_send()
-        if k < LINE - 1:
+        if k < last:
             pl.when(order[k] > z)(lambda: up(k).wait_send())
             pl.when(order[k] < z)(lambda: down(k).wait_send())
+            pl.when(order[k] > z)(lambda: up2(k).wait_send())
+            pl.when(order[k] < z)(lambda: down2(k).wait_send())
     done.wait()
 
 
@@ -464,7 +507,8 @@
             pltpu.VMEM((n_dp, rows, wide), bf),
             dma((3,)), dma((n_feat,)), dma(()),
             dma((3,)), dma((3,)), dma((LINE,)), dma((LINE,)), dma((LINE,)),
-            dma((2, LINE)), dma((2, LINE)), dma((2, LINE)), dma((2, LINE)),
+            dma((LINE,)), dma((LINE,)), dma((LINE,)),
+            dma((2, LINE)), dma((2, LINE)), dma((2,)), dma((2,)),
             dma((4, LINE)), dma((4, LINE)),
         ],
         compiler_params=pltpu.CompilerParams(
@@ -512,14 +556,17 @@
             pltpu.VMEM((2, local * units, wide), bf),
             pltpu.VMEM((2, LINE, n_dp, rows, wide), bf),
             pltpu.VMEM((LINE, n_dp, rows, wide), bf),
-            pltpu.VMEM((LINE, rows // 2, wide), bf),
-            pltpu.VMEM((LINE, rows // 2, wide), bf),
+            pltpu.VMEM((rows // 2, wide), bf),
+            pltpu.VMEM((rows // 2, wide), bf),
+            pltpu.VMEM((LINE, rows, wide), bf),
+            pltpu.VMEM((LINE, rows, wide), bf),
             pltpu.VMEM((LINE, rows, wide), bf),
             pltpu.VMEM((LINE, rows, wide), bf),
             pltpu.VMEM((LINE, rows, wide), bf),
             pltpu.VMEM((LINE, rows, wide), bf),
             dma(()), dma((2,)), dma((3,)), dma((3,)), dma((LINE,)), dma((LINE,)),
-            dma((2, LINE)), dma((2, LINE)), dma((2, LINE)), dma((2, LINE)),
+            dma((2,)), dma((2,)), dma((2, LINE)), dma((2, LINE)),
+            dma((LINE,)), dma((LINE,)), dma((LINE,)), dma((LINE,)),
             dma((LINE,)), dma((LINE,)), dma((LINE,)), dma((LINE,)),
         ],
         compiler_params=pltpu.CompilerParams(

time: 260 us -> 260 us (level)
    pallas_call x1, Pallas kernels: 101 us -> 115 us  [token_plan(): pl.pallas_call(scatter_kernel, out_shape=(jax.ShapeDtypeStruct((rows, wid...]
    pallas_call x1, Pallas kernels: 104 us -> 92.5 us  [token_plan(): pl.pallas_call(gather_kernel, out_shape=(jax.ShapeDtypeStruct((n_dp, n_fe...]
where the time goes in v3:
time: 260 us
  Pallas kernels  246 us (95%)
  local copies, waits for them, and re-layouts  11.7 us (4%)
    pallas_call x1, Pallas kernels, token_plan(): pl.pallas_call(scatter_kernel, out_shape=(jax.ShapeDtypeStruct((rows, wid...  115 us
    pallas_call x1, Pallas kernels, token_plan(): pl.pallas_call(gather_kernel, out_shape=(jax.ShapeDtypeStruct((n_dp, n_fe...  92.5 us
    pallas_call x1, Pallas kernels, token_plan(): pl.pallas_call(local_kernel, out_shape=(jax.ShapeDtypeStruct(cot_t.shape,...  38.6 us
    unnamed x14, local copies, waits for them, and re-layouts  9.24 us

profile of v3, /device:TPU:18, one launch (start us, length us, event | category | flops | bytes accessed | tf_op | source)
XLA Modules:
  0.0 259.5 jit_solution(9416266670441410650)
XLA Ops:
  0.6 0.8 copy.18.cols
  1.4 0.8 select_reduce_fusion.inv
  2.2 1.6 copy.15
  3.8 1.1 copy.22
  4.9 92.5 %gather.1 = (bf16[4,8,128,2048]{3,2,1,0:T(8,128)(2,1)}, bf16[4,32,32,128]{3,2,1,0:T(8,128)(2,1)}, bf16[8,1024,2048]{2,1,0:T(8,128)(2,1)}, f32[1024,512]{1,0:T(8,128)}) custom-call(bf16[128,2048]{1,0:T(8,128)(2,1)} %tokens.1, bf16[4,32,32,128]{3,2,1,0:T(8,128)(2,1)} %bitcast.8, s32[32,128]{1,0:T(8,128)} %select_reduce_fusion.inv, bf16[32,16,32,128]{3,2,1,0:T(8,128)(2,1)} %weight.1), custom_call_target="tpu_custom_call" | custom-call | tf_op jit(solution)/shard_map/gather/pallas_call | solution.py:494
  97.3 0.0 copy-start
  97.3 1.6 copy-done
  98.9 0.0 copy-start.1
  98.9 1.2 copy-done.1
  100.1 38.6 %local.1 = (bf16[4,32,32,128]{3,2,1,0:T(8,128)(2,1)S(1)}, bf16[32,16,32,128]{3,2,1,0:T(8,128)(2,1)}, bf16[512,1024]{1,0:T(8,128)(2,1)S(1)}) custom-call(s32[32,16]{1,0:T(8,128)S(1)} %copy.18.cols, bf16[4,8,128,2048]{3,2,1,0:T(8,128)(2,1)} %get-tuple-element.12.tok, f32[1024,512]{1,0:T(8,128)S(1)} %copy-done, bf16[4,32,32,128]{3,2,1,0:T(8,128)(2,1)S(1)} %copy-done.1), custom_call_target="tpu_custom_call" | custom-call | tf_op jit(solution)/shard_map/local/pallas_call | solution.py:521
  138.7 0.0 copy-start.2
  138.7 1.0 copy-done.2
  139.7 0.0 copy-start.3
  139.7 1.0 copy-done.3
  140.6 115.4 %scatter.1 = (bf16[128,2048]{1,0:T(8,128)(2,1)}, bf16[4,32,32,128]{3,2,1,0:T(8,128)(2,1)}) custom-call(bf16[512,1024]{1,0:T(8,128)(2,1)} %copy-done.3, bf16[8,1024,2048]{2,1,0:T(8,128)(2,1)} %get-tuple-element.16.wd, bf16[4,32,32,128]{3,2,1,0:T(8,128)(2,1)} %copy-done.2), custom_call_target="tpu_custom_call" | custom-call | tf_op jit(solution)/shard_map/scatter/pallas_call | solution.py:547
  256.0 0.0 copy-start.4
  256.0 1.4 copy.19
  257.4 1.3 copy.20
  258.7 0.0 copy-done.4
  258.7 0.8 copy.24
Async XLA Ops:
  97.3 1.6 copy-start
  98.9 1.2 copy-start.1
  138.7 1.0 copy-start.2
  139.7 1.0 copy-start.3
  256.0 2.7 %copy-start.4 = (bf16[128,2048]{1,0:T(8,128)(2,1)S(1)}, bf16[128,2048]{1,0:T(8,128)(2,1)}, u32[]{:S(2)}) copy-start(bf16[128,2048]{1,0:T(8,128)(2,1)} %get-tuple-element.31) | copy-start | bytes 1572868

commit v4 on v3

--- a/solution.py
+++ b/solution.py
@@ -203,7 +203,7 @@
     def goes_down(k):
         return jnp.logical_and(order[k] >= z, z > 0)
 
-    builds = ((0, 1, 2), (3, 4, 5), (6, 7))
+    builds = ((0, 1), (2, 3), (4, 5), (6, 7))
     for k in range(LINE + 3):
         if k < LINE:
             if k > 0:

time: 260 us -> 263 us (1.012)
  Pallas kernels: 246 us -> 249 us
    pallas_call x1, Pallas kernels: 92.5 us -> 96.1 us  [token_plan(): pl.pallas_call(gather_kernel, out_shape=(jax.ShapeDtypeStruct((n_dp, n_fe...]
where the time goes in v4:
time: 263 us; the launch traced here: 262 us
  Pallas kernels  249 us (95%)
  local copies, waits for them, and re-layouts  11.7 us (4%)
    pallas_call x1, Pallas kernels, token_plan(): pl.pallas_call(scatter_kernel, out_shape=(jax.ShapeDtypeStruct((rows, wid...  115 us
    pallas_call x1, Pallas kernels, token_plan(): pl.pallas_call(gather_kernel, out_shape=(jax.ShapeDtypeStruct((n_dp, n_fe...  96.1 us
    pallas_call x1, Pallas kernels, token_plan(): pl.pallas_call(local_kernel, out_shape=(jax.ShapeDtypeStruct(cot_t.shape,...  38.6 us
    unnamed x14, local copies, waits for them, and re-layouts  9.24 us

profile of v4, /device:TPU:18, one launch (start us, length us, event | category | flops | bytes accessed | tf_op | source)
XLA Modules:
  0.0 262.5 jit_solution(15769239688455871626)
XLA Ops:
  0.6 0.8 copy.18.cols
  1.4 0.8 select_reduce_fusion.inv
  2.2 1.6 copy.15
  3.8 1.1 copy.22
  4.9 96.1 %gather.1 = (bf16[4,8,128,2048]{3,2,1,0:T(8,128)(2,1)}, bf16[4,32,32,128]{3,2,1,0:T(8,128)(2,1)}, bf16[8,1024,2048]{2,1,0:T(8,128)(2,1)}, f32[1024,512]{1,0:T(8,128)}) custom-call(bf16[128,2048]{1,0:T(8,128)(2,1)} %tokens.1, bf16[4,32,32,128]{3,2,1,0:T(8,128)(2,1)} %bitcast.8, s32[32,128]{1,0:T(8,128)} %select_reduce_fusion.inv, bf16[32,16,32,128]{3,2,1,0:T(8,128)(2,1)} %weight.1), custom_call_target="tpu_custom_call" | custom-call | tf_op jit(solution)/shard_map/gather/pallas_call | solution.py:494
  101.0 0.0 copy-start
  101.0 1.6 copy-done
  102.6 0.0 copy-start.1
  102.6 1.2 copy-done.1
  103.8 38.6 %local.1 = (bf16[4,32,32,128]{3,2,1,0:T(8,128)(2,1)S(1)}, bf16[32,16,32,128]{3,2,1,0:T(8,128)(2,1)}, bf16[512,1024]{1,0:T(8,128)(2,1)S(1)}) custom-call(s32[32,16]{1,0:T(8,128)S(1)} %copy.18.cols, bf16[4,8,128,2048]{3,2,1,0:T(8,128)(2,1)} %get-tuple-element.12.tok, f32[1024,512]{1,0:T(8,128)S(1)} %copy-done, bf16[4,32,32,128]{3,2,1,0:T(8,128)(2,1)S(1)} %copy-done.1), custom_call_target="tpu_custom_call" | custom-call | tf_op jit(solution)/shard_map/local/pallas_call | solution.py:521
  142.4 0.0 copy-start.2
  142.4 1.0 copy-done.2
  143.4 0.0 copy-start.3
  143.4 1.0 copy-done.3
  144.4 114.5 %scatter.1 = (bf16[128,2048]{1,0:T(8,128)(2,1)}, bf16[4,32,32,128]{3,2,1,0:T(8,128)(2,1)}) custom-call(bf16[512,1024]{1,0:T(8,128)(2,1)} %copy-done.3, bf16[8,1024,2048]{2,1,0:T(8,128)(2,1)} %get-tuple-element.16.wd, bf16[4,32,32,128]{3,2,1,0:T(8,128)(2,1)} %copy-done.2), custom_call_target="tpu_custom_call" | custom-call | tf_op jit(solution)/shard_map/scatter/pallas_call | solution.py:547
  258.9 0.0 copy-start.4
  258.9 1.4 copy.19
  260.4 1.3 copy.20
  261.7 0.0 copy-done.4
  261.7 0.8 copy.24
Async XLA Ops:
  101.0 1.6 copy-start
  102.6 1.2 copy-start.1
  142.4 1.0 copy-start.2
  143.4 1.0 copy-start.3
  258.9 2.7 %copy-start.4 = (bf16[128,2048]{1,0:T(8,128)(2,1)S(1)}, bf16[128,2048]{1,0:T(8,128)(2,1)}, u32[]{:S(2)}) copy-start(bf16[128,2048]{1,0:T(8,128)(2,1)} %get-tuple-element.31) | copy-start | bytes 1572868
